TPU v7x, 32 devices: a whole 2x2x4 slice. The times are simulated.
32 devices in a mesh: gx: 8 (over z, core), gy: 4 (over y, x).
Axes of the slice: x: 2, y: 2, z: 4, core: 2. Of those that a mesh axis runs over, the one named last changes fastest.
Arguments:
- patches: bfloat16 [8, 64, 128, 512], P(None, None, 'gx', 'gy'), may hold values from -6 to 6
- patch_wx: bfloat16 [8, 4, 128], P(None, 'gy', 'gx'), may hold values from 1 to 3
- patch_wy: bfloat16 [8, 8, 512], P(None, 'gx', 'gy'), may hold values from 1 to 3
- offset_x: int32 [8, 8, 4], P(None, 'gx', 'gy'), may hold values from 0 to 15
- offset_y: int32 [8, 8, 4], P(None, 'gx', 'gy'), may hold values from 0 to 127
- block_counts: int32 [8, 4], P('gx', 'gy'), may hold values from 2 to 8, as said below
- template: bfloat16 [64, 128, 512], P(None, 'gx', 'gy'), may hold values from -6 to 6
- stiff_mu: float32 [64, 128, 512], P(None, 'gx', 'gy'), may hold values from 0.5 to 2
- stiff_lam: float32 [64, 128, 512], P(None, 'gx', 'gy'), may hold values from 0.5 to 4
- start_field: float32 [3, 64, 128, 512], P(None, None, 'gx', 'gy'), may hold values from -4 to 4
Outputs:
- joined: bfloat16 [64, 128, 512], P(None, 'gx', 'gy')
- field: float32 [3, 64, 128, 512], P(None, None, 'gx', 'gy')
Inputs may be any that keep to these rules, and one draw needn't show every extreme that they name: `block_counts`: a block's patch slots at or beyond its count are unused; some block holds exactly 8 live patches.
All inputs are finite; a program needn't handle non-finite values.
Results may differ from a plain program's by a relative error of at most 0.0045.
Values may be sent and summed in bfloat16 or wider, within the bound.
A program may use at most 128 MiB of HBM per device.

v0:
```python
import functools

import jax
import jax.numpy as jnp
from jax import lax
from jax.experimental import pallas as pl
from jax.experimental.pallas import tpu as pltpu
from jax.sharding import PartitionSpec as P

PASSES = 4
RELAX_FACTOR = 0.9
F32 = jnp.float32
BF16 = jnp.bfloat16
MESH = pl.DeviceIdType.MESH
DIRS = ((1, 0), (-1, 0), (0, 1), (0, -1), (1, 1), (1, -1), (-1, 1), (-1, -1))
CHUNKS = 4
GROUP = 8


def blend_kernel(count, ox_ref, oy_ref, wx_ref, patches, wy_ref, q00, qx, q01, wout, canvas, wcan, res):
    rows, by = patches.shape[1:]
    bx, depth = q00.shape[:2]
    canvas[...] = jnp.zeros_like(canvas)
    wcan[...] = jnp.zeros_like(wcan)
    source = lax.broadcasted_iota(jnp.int32, (by, 2 * by), 0)
    target = lax.broadcasted_iota(jnp.int32, (by, 2 * by), 1)

    def add_patch(s, carry):
        ox = ox_ref[s, 0]
        place = jnp.where(target == source + oy_ref[s, 0], 1.0, 0.0).astype(BF16)
        moved = jnp.dot(patches[s], place, preferred_element_type=F32)
        res[0] = moved[:, :by]
        res[1] = moved[:, by:]
        along_y = jnp.broadcast_to(wy_ref[s].astype(F32), (16, by)).astype(BF16)
        wy_row = jnp.dot(along_y, place, preferred_element_type=F32)[:8]
        for x in range(bx):
            wx = wx_ref[s, x]
            for h in range(2):
                weight = wx * wy_row[:, h * by : (h + 1) * by]
                canvas[h, ox + x] += res[h, pl.ds(x, depth, stride=bx), :] * weight[0:1]
                wcan[h, ox + x] += weight
        return carry

    lax.fori_loop(0, count[0, 0], add_patch, 0)
    q00[...] = canvas[0, :bx]
    qx[:, 0] = canvas[0, bx:].astype(BF16)
    qx[:, 1] = canvas[1, bx:].astype(BF16)
    q01[...] = canvas[1, :bx].astype(BF16)
    for x in range(bx):
        wout[0, x : x + 1] = wcan[0, x, 0:1]
        wout[1, x : x + 1] = wcan[0, bx + x, 0:1]
        wout[2, x : x + 1] = wcan[1, bx + x, 0:1]
        wout[3, x : x + 1] = wcan[1, x, 0:1]


def relax_kernel(
    q00, qx, q01, wq, tmpl, mu_ref, lam_ref, fld, jout, fout,
    field, mu, qb, coef, force, joined, tall, grad, acc, packed, cpack, wsum,
    land_q, land_w, sy, sw, land_y, land_wy,
    xs, xl, ap, al, dl, cxs, cxl, cap, cal, jxs, jxl, jap, jal,
    send_sem, recv_sem,
):
    bx, depth, by = q00.shape
    gx, gy = lax.axis_index("gx"), lax.axis_index("gy")
    nx, ny = lax.axis_size("gx"), lax.axis_size("gy")

    def exists(d):
        ok = True
        for where, step, count in ((gx, d[0], nx), (gy, d[1], ny)):
            if step == 1:
                ok = jnp.logical_and(ok, where < count - 1)
            if step == -1:
                ok = jnp.logical_and(ok, where > 0)
        return ok

    def opposite(d):
        return (-d[0], -d[1])

    pending = []

    def rdma(src, dst, idx, d):
        return pltpu.make_async_remote_copy(
            src_ref=src, dst_ref=dst, send_sem=send_sem.at[idx], recv_sem=recv_sem.at[idx],
            device_id=(gx + d[0], gy + d[1]), device_id_type=MESH,
        )

    counter = [0]

    def send(src, dst, d):
        idx = counter[0]
        counter[0] += 1

        @pl.when(exists(d))
        def _():
            rdma(src, dst, idx, d).start()

        pending.append((src, dst, idx, d))

        def arrive():
            @pl.when(exists(opposite(d)))
            def _():
                rdma(src, dst, idx, d).wait_recv()

        return arrive

    lane = lax.broadcasted_iota(jnp.int32, (depth, by), 1)
    level = lax.broadcasted_iota(jnp.int32, (depth, by), 0)
    pos = lax.rem(lane, GROUP)

    def strided(x):
        return pl.ds(x, depth, stride=bx)

    def z_next(v):
        return jnp.where(level == depth - 1, 0.0, pltpu.roll(v, depth - 1, 0))

    def z_prev(v):
        return jnp.where(level == 0, 0.0, pltpu.roll(v, 1, 0))

    def y_next(v, edge):
        return jnp.where(lane == by - 1, edge, pltpu.roll(v, by - 1, 1))

    def y_prev(v, edge):
        return jnp.where(lane == 0, edge, pltpu.roll(v, 1, 1))

    def at_edge(pack, x):
        return pltpu.roll(pack, by - 4 - GROUP * x, 1)

    def pack_in(slot, plane, x):
        own = jnp.logical_and(lane >= GROUP * x, lane < GROUP * x + 4)
        acc[slot] = jnp.where(own, pltpu.roll(plane, GROUP * x + 2, 1), acc[slot])

    def merge(own, left, right):
        left, right = left.astype(F32), right.astype(F32)
        out = jnp.where(pos >= 6, pltpu.roll(own, 4, 1), own)
        out = jnp.where(pos == 2, pltpu.roll(left, 2, 1), out)
        out = jnp.where(pos == 4, pltpu.roll(left, 3, 1), out)
        out = jnp.where(pos == 3, pltpu.roll(right, 1, 1), out)
        return jnp.where(pos == 5, pltpu.roll(right, 2, 1), out)

    barrier = pltpu.get_barrier_semaphore()
    total = 0
    for d in DIRS:
        @pl.when(exists(d))
        def _(d=d):
            pl.semaphore_signal(barrier, inc=1, device_id=(gx + d[0], gy + d[1]), device_id_type=MESH)

        total = total + jnp.where(exists(d), 1, 0)
    pl.semaphore_wait(barrier, total)

    step = bx // CHUNKS
    got_q = []
    for c in range(CHUNKS):
        part = pl.ds(c * step, step)
        got_q.append(send(qx.at[part], land_q.at[part], (1, 0)))
    got_w = send(wq.at[pl.ds(1, 2)], land_w, (1, 0))

    for k, d in enumerate(DIRS):
        @pl.when(jnp.logical_not(exists(opposite(d))))
        def _(k=k):
            if k == 0:
                land_q[...] = jnp.zeros_like(land_q)
                land_w[...] = jnp.zeros_like(land_w)
            if k == 2:
                land_y[...] = jnp.zeros_like(land_y)
                land_wy[...] = jnp.zeros_like(land_wy)
            if k < 2:
                for p in range(PASSES):
                    xl[p, k] = jnp.zeros(xl.shape[2:], BF16)
                cxl[k] = jnp.zeros(cxl.shape[1:], BF16)
                jxl[k] = jnp.zeros(jxl.shape[1:], BF16)
            elif k < 4:
                for p in range(PASSES):
                    al[p, k - 2] = jnp.zeros(al.shape[2:], BF16)
                cal[k - 2] = jnp.zeros(cal.shape[1:], BF16)
                jal[k - 2] = jnp.zeros(jal.shape[1:], BF16)
            else:
                for p in range(PASSES):
                    dl[p, k - 4] = jnp.zeros(dl.shape[2:], BF16)

    acc[...] = jnp.zeros_like(acc)

    def load(x, carry):
        for c in range(3):
            plane = fld[c, strided(x), :]
            field[0, c, x + 2] = plane
            pack_in(c, plane, x)
        mu_plane = mu_ref[strided(x), :]
        bulk = lam_ref[strided(x), :] + mu_plane
        mu[x + 1] = mu_plane
        qb[x + 1] = bulk
        pack_in(3, mu_plane, x)
        pack_in(4, bulk, x)
        return carry

    lax.fori_loop(0, bx, load, 0)

    def send_field(p, b):
        for c in range(3):
            xs[p, 0, c] = field[b, c, bx : bx + 2].astype(BF16)
            xs[p, 1, c] = field[b, c, 2:4].astype(BF16)
            ap[p, c] = acc[c].astype(BF16)
        got = [send(xs.at[p, k], xl.at[p, k], DIRS[k]) for k in range(2)]
        got += [send(ap.at[p], al.at[p, k - 2], DIRS[k]) for k in range(2, 4)]
        got += [send(ap.at[p, pl.ds(1, 2)], dl.at[p, k - 4], DIRS[k]) for k in range(4, 8)]
        return got

    got_field = send_field(0, 0)
    for k, at in ((0, bx), (1, 1)):
        cxs[k, 0] = mu[at].astype(BF16)
        cxs[k, 1] = qb[at].astype(BF16)
    cap[...] = acc[3:5].astype(BF16)
    got_coef = [send(cxs.at[k], cxl.at[k], DIRS[k]) for k in range(2)]
    got_coef += [send(cap, cal.at[k - 2], DIRS[k]) for k in range(2, 4)]

    got_w()
    sw[...] = wq[3] + land_w[1]
    got_wy = send(sw, land_wy, (0, 1))
    got_y = []
    for c in range(CHUNKS):
        part = pl.ds(c * step, step)
        got_q[c]()
        sy[part] = (q01[part].astype(F32) + land_q[part, 1].astype(F32)).astype(BF16)
        got_y.append(send(sy.at[part], land_y.at[part], (0, 1)))

    for arrive in got_coef:
        arrive()
    for k, at in ((0, 0), (1, bx + 1)):
        mu[at] = cxl[k, 0].astype(F32)
        qb[at] = cxl[k, 1].astype(F32)
    for c in range(2):
        cpack[c] = merge(acc[3 + c], cal[0, c], cal[1, c])
    cpack[1] = 0.25 * cpack[1]

    def coefficients(x, carry):
        here = mu[x + 1]
        rate = RELAX_FACTOR / (6.0 * here + 3.0 * qb[x + 1])
        half = 0.5 * rate
        edge = at_edge(cpack[0], x)
        near = (
            z_next(here), z_prev(here), mu[x + 2], mu[x], y_next(here, edge), y_prev(here, edge),
        )
        rest = 1.0
        for n, other in enumerate(near):
            one = half * (here + other)
            coef[n, x] = one
            rest = rest - one
        coef[6, x] = rest
        coef[7, x] = rate
        return carry

    lax.fori_loop(0, bx, coefficients, 0)

    def scale(x, carry):
        qb[x] = 0.25 * qb[x]
        return carry

    lax.fori_loop(0, bx + 2, scale, 0)

    def relax(p, got):
        b, nb = p % 2, 1 - p % 2
        last = p == PASSES - 1
        for arrive in got:
            arrive()
        for c in range(3):
            field[b, c, 0:2] = xl[p, 0, c].astype(F32)
            field[b, c, bx + 2 : bx + 4] = xl[p, 1, c].astype(F32)
            packed[c] = merge(acc[c], al[p, 0, c], al[p, 1, c])
        corner = [[dl[p, k, c].astype(F32) for c in range(2)] for k in range(4)]
        top = GROUP * (bx - 1)

        def bring(k, c, at):
            plus_x, plus_y = DIRS[4 + k]
            source = (top if plus_x == 1 else 0) + (1 if plus_y == 1 else 2)
            return pltpu.roll(corner[k][c], (at - source) % by, 1)

        def edge_corners(low, high):
            return jnp.where(lane == 0, bring(low, 1, 0), bring(high, 1, by - 1))

        vx = packed[1]
        ahead = pltpu.roll(vx, by - GROUP, 1)
        ahead = jnp.where(lane == top + 3, bring(3, 0, top + 3), ahead)
        ahead = jnp.where(lane == top + 4, bring(2, 0, top + 4), ahead)
        behind = pltpu.roll(vx, GROUP, 1)
        behind = jnp.where(lane == 3, bring(1, 0, 3), behind)
        behind = jnp.where(lane == 4, bring(0, 0, 4), behind)
        if GROUP * bx < by:
            ahead = jnp.where(lane >= GROUP * bx, 0.0, ahead)
        vz, vy = packed[0], packed[2]
        packed[3] = cpack[1] * (
            (ahead - behind) + (z_next(vz) - z_prev(vz))
            + (pltpu.roll(vy, by - 2, 1) - pltpu.roll(vy, 2, 1))
        )

        def gradient(at, edge):
            vz, vy = field[b, 0, at + 1], field[b, 2, at + 1]
            grad[at] = qb[at] * (
                (field[b, 1, at + 2] - field[b, 1, at])
                + (z_next(vz) - z_prev(vz))
                + (y_next(vy, edge) - y_prev(vy, edge))
            )

        gradient(0, edge_corners(0, 1))
        gradient(bx + 1, edge_corners(2, 3))

        def inner(x, carry):
            gradient(x + 1, at_edge(packed[2], x))
            return carry

        lax.fori_loop(0, bx, inner, 0)
        if not last:
            acc[0:3] = jnp.zeros((3, depth, by), F32)

        def update(x, carry):
            g = grad[x + 1]
            g_edge = at_edge(packed[3], x)
            rise = (
                z_next(g) - z_prev(g),
                grad[x + 2] - grad[x],
                y_next(g, g_edge) - y_prev(g, g_edge),
            )
            k = [coef[n, x] for n in range(8)]
            for c in range(3):
                v = field[b, c, x + 2]
                edge = at_edge(packed[c], x)
                new = k[6] * v + k[7] * rise[c]
                new = new + k[0] * z_next(v) + k[1] * z_prev(v)
                new = new + k[2] * field[b, c, x + 3] + k[3] * field[b, c, x + 1]
                new = new + k[4] * y_next(v, edge) + k[5] * y_prev(v, edge)
                if p > 0:
                    new = new + force[c, x]
                if last:
                    fout[c, strided(x), :] = new
                else:
                    field[nb, c, x + 2] = new
                    if p > 0:
                        pack_in(c, new, x)
            return carry

        lax.fori_loop(0, bx, update, 0)

    relax(0, got_field)

    got_wy()
    wsum[...] = jnp.maximum(wq[0] + land_w[0] + land_wy[...], 1.0)
    acc[3] = jnp.zeros((depth, by), F32)
    tall[...] = tmpl[...].astype(F32)

    def join(x, carry):
        value = q00[x] + land_q[x, 0].astype(F32) + land_y[x].astype(F32)
        plane = (value / wsum[pl.ds(x, 1), :]).astype(BF16).astype(F32)
        joined[x + 1] = plane
        pack_in(3, plane, x)
        return carry

    for c in range(CHUNKS):
        got_y[c]()
        lax.fori_loop(c * step, (c + 1) * step, join, 0)
    jxs[0] = joined[bx].astype(BF16)
    jxs[1] = joined[1].astype(BF16)
    jap[...] = acc[3].astype(BF16)
    got = [send(jxs.at[k], jxl.at[k], DIRS[k]) for k in range(2)]
    got += [send(jap, jal.at[k - 2], DIRS[k]) for k in range(2, 4)]
    for arrive in got:
        arrive()
    joined[0] = jxl[0].astype(F32)
    joined[bx + 1] = jxl[1].astype(F32)
    cpack[0] = merge(acc[3], jal[0], jal[1])

    def forcing(x, carry):
        here = joined[x + 1]
        edge = at_edge(cpack[0], x)
        mismatch = (tall[strided(x), :] - here) * 0.5 * coef[7, x]
        tall[strided(x), :] = here
        slopes = (
            z_next(here) - z_prev(here),
            joined[x + 2] - joined[x],
            y_next(here, edge) - y_prev(here, edge),
        )
        for c in range(3):
            one = mismatch * slopes[c]
            force[c, x] = one
            new = field[1, c, x + 2] + one
            field[1, c, x + 2] = new
            pack_in(c, new, x)
        return carry

    lax.fori_loop(0, bx, forcing, 0)
    got_field = send_field(1, 1)
    jout[...] = tall[...].astype(BF16)
    for p in range(1, PASSES):
        relax(p, got_field)
        if p < PASSES - 1:
            got_field = send_field(p + 1, (p + 1) % 2)
    for src, dst, idx, d in pending:
        @pl.when(exists(d))
        def _(src=src, dst=dst, idx=idx, d=d):
            rdma(src, dst, idx, d).wait_send()


def per_device(
    patches, patch_wx, patch_wy, offset_x, offset_y, block_counts, template, stiff_mu, stiff_lam, start_field
):
    slots, depth, bx, by = patches.shape
    vmem = pl.BlockSpec(memory_space=pltpu.VMEM)
    smem = pl.BlockSpec(memory_space=pltpu.SMEM)
    plane = (depth, by)
    shape = jax.ShapeDtypeStruct
    quads = pl.pallas_call(
        blend_kernel,
        out_shape=(
            shape((bx,) + plane, F32),
            shape((bx, 2) + plane, BF16),
            shape((bx,) + plane, BF16),
            shape((4, bx, by), F32),
        ),
        in_specs=[smem] * 4 + [vmem] * 2,
        out_specs=(vmem,) * 4,
        scratch_shapes=[
            pltpu.VMEM((2, 2 * bx) + plane, F32),
            pltpu.VMEM((2, 2 * bx, 8, by), F32),
            pltpu.VMEM((2, depth * bx, by), F32),
        ],
        compiler_params=pltpu.CompilerParams(vmem_limit_bytes=40 * 2**20),
        name="blend",
    )(
        block_counts,
        offset_x.reshape(slots, 1),
        offset_y.reshape(slots, 1),
        patch_wx.reshape(slots, bx).astype(F32),
        patches.reshape(slots, depth * bx, by),
        patch_wy,
    )
    n_copies = CHUNKS + 1 + 8 + 4 + 1 + CHUNKS + 4 + 8 * (PASSES - 1)
    scratch = [
        ((2, 3, bx + 4) + plane, F32),
        ((bx + 2,) + plane, F32),
        ((bx + 2,) + plane, F32),
        ((8, bx) + plane, F32),
        ((3, bx) + plane, F32),
        ((bx + 2,) + plane, F32),
        ((depth * bx, by), F32),
        ((bx + 2,) + plane, F32),
        ((5,) + plane, F32),
        ((4,) + plane, F32),
        ((2,) + plane, F32),
        ((bx, by), F32),
        ((bx, 2) + plane, BF16),
        ((2, bx, by), F32),
        ((bx,) + plane, BF16),
        ((bx, by), F32),
        ((bx,) + plane, BF16),
        ((bx, by), F32),
        ((PASSES, 2, 3, 2) + plane, BF16),
        ((PASSES, 2, 3, 2) + plane, BF16),
        ((PASSES, 3) + plane, BF16),
        ((PASSES, 2, 3) + plane, BF16),
        ((PASSES, 4, 2) + plane, BF16),
        ((2, 2) + plane, BF16),
        ((2, 2) + plane, BF16),
        ((2,) + plane, BF16),
        ((2, 2) + plane, BF16),
        ((2,) + plane, BF16),
        ((2,) + plane, BF16),
        (plane, BF16),
        ((2,) + plane, BF16),
    ]
    joined, field = pl.pallas_call(
        relax_kernel,
        out_shape=(shape((depth * bx, by), BF16), shape((3, depth * bx, by), F32)),
        in_specs=[vmem] * 8,
        out_specs=(vmem, vmem),
        scratch_shapes=[pltpu.VMEM(dims, kind) for dims, kind in scratch]
        + [pltpu.SemaphoreType.DMA((n_copies,)), pltpu.SemaphoreType.DMA((n_copies,))],
        compiler_params=pltpu.CompilerParams(
            collective_id=0, has_side_effects=True, vmem_limit_bytes=50 * 2**20
        ),
        name="relax",
    )(
        *quads,
        template.reshape(depth * bx, by),
        stiff_mu.reshape(depth * bx, by),
        stiff_lam.reshape(depth * bx, by),
        start_field.reshape(3, depth * bx, by),
    )
    return joined.reshape(depth, bx, by), field.reshape(3, depth, bx, by)


def solution(mesh):
    placed = (
        P(None, None, "gx", "gy"),
        P(None, "gy", "gx"),
        P(None, "gx", "gy"),
        P(None, "gx", "gy"),
        P(None, "gx", "gy"),
        P("gx", "gy"),
        P(None, "gx", "gy"),
        P(None, "gx", "gy"),
        P(None, "gx", "gy"),
        P(None, None, "gx", "gy"),
    )
    return jax.shard_map(
        per_device,
        mesh=mesh,
        in_specs=placed,
        out_specs=(P(None, "gx", "gy"), P(None, None, "gx", "gy")),
        check_vma=False,
    )
```

profile of v0, /device:TPU:0, one launch (start us, length us, event | category | flops | bytes accessed | tf_op | source)
XLA Modules:
  0.0 83.7 jit_solution(5349904840408872816)
XLA Ops:
  1.3 0.7 bitcast_convert_fusion.wx_ref
  2.0 0.7 copy.14.wy_ref
  2.6 0.7 copy.12.ox_ref
  3.4 0.7 copy.13.oy_ref
  4.1 0.0 copy-start
  4.1 1.6 %copy-done = bf16[8,64,16,128]{3,2,1,0:T(8,128)(2,1)S(1)} copy-done((bf16[8,64,16,128]{3,2,1,0:T(8,128)(2,1)S(1)}, bf16[8,64,16,128]{3,2,1,0:T(8,128)(2,1)}, u32[]{:S(2)}) %copy-start) | copy-done | bytes 2097176
  5.7 0.0 copy-start.1
  5.7 0.0 copy-start.2
  5.7 0.0 copy-start.3
  5.7 2.5 %blend.1 = (f32[16,64,128]{2,1,0:T(8,128)S(1)}, bf16[16,2,64,128]{3,2,1,0:T(8,128)(2,1)S(1)}, bf16[16,64,128]{2,1,0:T(8,128)(2,1)S(1)}, f32[4,16,128]{2,1,0:T(8,128)S(1)}) custom-call(s32[1,1]{1,0:T(1,128)S(6)} %copy.17.count, s32[8,1]{1,0:T(8,128)S(1)} %copy.12.ox_ref, s32[8,1]{1,0:T(8,128)S(1)} %copy.13.oy_ref, f32[8,16]{1,0:T(8,128)S(1)} %bitcast_convert_fusion.wx_ref, ...), custom_call_target="tpu_custom_call" | custom-call | tf_op jit(solution)/shard_map/blend/pallas_call | solution.py:408
  8.2 0.0 copy-done.1
  8.2 0.0 copy-done.2
  8.2 0.0 copy-done.3
  8.2 72.0 %relax.1 = (bf16[1024,128]{1,0:T(8,128)(2,1)S(1)}, f32[3,1024,128]{2,1,0:T(8,128)}) custom-call(f32[16,64,128]{2,1,0:T(8,128)S(1)} %get-tuple-element.8.q00, bf16[16,2,64,128]{3,2,1,0:T(8,128)(2,1)S(1)} %get-tuple-element.9.qx, bf16[16,64,128]{2,1,0:T(8,128)(2,1)S(1)} %get-tuple-element.10.q01, f32[4,16,128]{2,1,0:T(8,128)S(1)} %get-tuple-element.11.wq, ...), custom_call_target="tpu_custom_call" | custom-call | tf_op jit(solution)/shard_map/relax/pallas_call | solution.py:467
  80.3 0.7 copy.18
  81.0 2.7 %copy.19 = f32[3,64,16,128]{3,2,1,0:T(8,128)} copy(f32[3,64,16,128]{3,2,1,0:T(8,128)} %bitcast.18) | data formatting | bytes 3145728
Async XLA Ops:
  4.1 1.6 %copy-start = (bf16[8,64,16,128]{3,2,1,0:T(8,128)(2,1)S(1)}, bf16[8,64,16,128]{3,2,1,0:T(8,128)(2,1)}, u32[]{:S(2)}) copy-start(bf16[8,64,16,128]{3,2,1,0:T(8,128)(2,1)} %param.10) | copy-start | bytes 6291460
  5.7 2.5 %copy-start.1 = (f32[64,16,128]{2,1,0:T(8,128)S(1)}, f32[64,16,128]{2,1,0:T(8,128)}, u32[]{:S(2)}) copy-start(f32[64,16,128]{2,1,0:T(8,128)} %param.17) | copy-start | bytes 1572868
  5.7 2.5 %copy-start.2 = (f32[64,16,128]{2,1,0:T(8,128)S(1)}, f32[64,16,128]{2,1,0:T(8,128)}, u32[]{:S(2)}) copy-start(f32[64,16,128]{2,1,0:T(8,128)} %param.18) | copy-start | bytes 1572868
  5.7 2.5 %copy-start.3 = (bf16[64,16,128]{2,1,0:T(8,128)(2,1)S(1)}, bf16[64,16,128]{2,1,0:T(8,128)(2,1)}, u32[]{:S(2)}) copy-start(bf16[64,16,128]{2,1,0:T(8,128)(2,1)} %param.16) | copy-start | bytes 786436
where the time goes:
time: 83.6 us; the launch traced here: 83.7 us
  Pallas kernels  74.5 us (89%)
  local copies, waits for them, and re-layouts  7.1 us (8%)
  between operations  1.32 us (2%)
    pallas_call x1, Pallas kernels, per_device(): pl.pallas_call(relax_kernel, out_shape=(shape((depth * bx, by), BF16), sh...  72 us
    unnamed x11, local copies, waits for them, and re-layouts  5.64 us
    pallas_call x1, Pallas kernels, per_device(): pl.pallas_call(blend_kernel, out_shape=(shape((bx,) + plane, F32), shape(...  2.5 us

commit v1 on v0

--- a/solution.py
+++ b/solution.py
@@ -17,31 +17,43 @@
 GROUP = 8
 
 
-def blend_kernel(count, ox_ref, oy_ref, wx_ref, patches, wy_ref, q00, qx, q01, wout, canvas, wcan, res):
-    rows, by = patches.shape[1:]
+def blend_kernel(count, table, patches, wy_ref, q00, qx, q01, wout, canvas, wcan, res, held, arrived):
+    by = held.shape[-1]
     bx, depth = q00.shape[:2]
+    live = count[0, 0]
+
+    def fetch(s):
+        return pltpu.make_async_copy(patches.at[s], held.at[s], arrived.at[s])
+
+    def begin(s, carry):
+        fetch(s).start()
+        return carry
+
+    lax.fori_loop(0, live, begin, 0)
     canvas[...] = jnp.zeros_like(canvas)
     wcan[...] = jnp.zeros_like(wcan)
     source = lax.broadcasted_iota(jnp.int32, (by, 2 * by), 0)
     target = lax.broadcasted_iota(jnp.int32, (by, 2 * by), 1)
 
     def add_patch(s, carry):
-        ox = ox_ref[s, 0]
-        place = jnp.where(target == source + oy_ref[s, 0], 1.0, 0.0).astype(BF16)
-        moved = jnp.dot(patches[s], place, preferred_element_type=F32)
+        ox = table[s, 0].astype(jnp.int32)
+        oy = table[s, 1].astype(jnp.int32)
+        place = jnp.where(target == source + oy, 1.0, 0.0).astype(BF16)
+        fetch(s).wait()
+        moved = jnp.dot(held[s], place, preferred_element_type=F32)
         res[0] = moved[:, :by]
         res[1] = moved[:, by:]
         along_y = jnp.broadcast_to(wy_ref[s].astype(F32), (16, by)).astype(BF16)
         wy_row = jnp.dot(along_y, place, preferred_element_type=F32)[:8]
         for x in range(bx):
-            wx = wx_ref[s, x]
+            wx = table[s, 2 + x]
             for h in range(2):
                 weight = wx * wy_row[:, h * by : (h + 1) * by]
                 canvas[h, ox + x] += res[h, pl.ds(x, depth, stride=bx), :] * weight[0:1]
                 wcan[h, ox + x] += weight
         return carry
 
-    lax.fori_loop(0, count[0, 0], add_patch, 0)
+    lax.fori_loop(0, live, add_patch, 0)
     q00[...] = canvas[0, :bx]
     qx[:, 0] = canvas[0, bx:].astype(BF16)
     qx[:, 1] = canvas[1, bx:].astype(BF16)
@@ -125,9 +137,20 @@
     def at_edge(pack, x):
         return pltpu.roll(pack, by - 4 - GROUP * x, 1)
 
-    def pack_in(slot, plane, x):
-        own = jnp.logical_and(lane >= GROUP * x, lane < GROUP * x + 4)
-        acc[slot] = jnp.where(own, pltpu.roll(plane, GROUP * x + 2, 1), acc[slot])
+    def pack_in(slot, planes, x0):
+        out = acc[slot]
+        for u, plane in enumerate(planes):
+            at = GROUP * (x0 + u)
+            own = jnp.logical_and(lane >= at, lane < at + 4)
+            out = jnp.where(own, pltpu.roll(plane, (at + 2) % by, 1), out)
+        acc[slot] = out
+
+    def pairs(low, high, body):
+        def two(n, carry):
+            body(2 * n)
+            return carry
+
+        lax.fori_loop(low // 2, high // 2, two, 0)
 
     def merge(own, left, right):
         left, right = left.astype(F32), right.astype(F32)
@@ -179,32 +202,36 @@
 
     acc[...] = jnp.zeros_like(acc)
 
-    def load(x, carry):
-        for c in range(3):
-            plane = fld[c, strided(x), :]
-            field[0, c, x + 2] = plane
-            pack_in(c, plane, x)
-        mu_plane = mu_ref[strided(x), :]
-        bulk = lam_ref[strided(x), :] + mu_plane
-        mu[x + 1] = mu_plane
-        qb[x + 1] = bulk
-        pack_in(3, mu_plane, x)
-        pack_in(4, bulk, x)
-        return carry
-
-    lax.fori_loop(0, bx, load, 0)
-
-    def send_field(p, b):
+    def load(x0):
+        span = (x0, x0 + 1)
+        planes = [[fld[c, strided(x), :] for x in span] for c in range(3)]
+        mus = [mu_ref[strided(x), :] for x in span]
+        bulks = [lam_ref[strided(x), :] + one for x, one in zip(span, mus)]
+        for u, x in enumerate(span):
+            for c in range(3):
+                field[0, c, x + 2] = planes[c][u]
+            mu[x + 1] = mus[u]
+            qb[x + 1] = bulks[u]
+        for slot, values in enumerate(planes + [mus, bulks]):
+            pack_in(slot, values, x0)
+
+    pairs(0, bx, load)
+
+    def send_planes(p, b):
         for c in range(3):
             xs[p, 0, c] = field[b, c, bx : bx + 2].astype(BF16)
             xs[p, 1, c] = field[b, c, 2:4].astype(BF16)
+        return [send(xs.at[p, k], xl.at[p, k], DIRS[k]) for k in range(2)]
+
+    def send_packs(p):
+        for c in range(3):
             ap[p, c] = acc[c].astype(BF16)
-        got = [send(xs.at[p, k], xl.at[p, k], DIRS[k]) for k in range(2)]
-        got += [send(ap.at[p], al.at[p, k - 2], DIRS[k]) for k in range(2, 4)]
-        got += [send(ap.at[p, pl.ds(1, 2)], dl.at[p, k - 4], DIRS[k]) for k in range(4, 8)]
-        return got
-
-    got_field = send_field(0, 0)
+        far = [send(ap.at[p, pl.ds(1, 2)], dl.at[p, k - 4], DIRS[k]) for k in range(4, 8)]
+        near = [send(ap.at[p], al.at[p, k - 2], DIRS[k]) for k in range(2, 4)]
+        return near, far
+
+    got_planes = send_planes(0, 0)
+    got_packs = send_packs(0)
     for k, at in ((0, bx), (1, 1)):
         cxs[k, 0] = mu[at].astype(BF16)
         cxs[k, 1] = qb[at].astype(BF16)
@@ -231,24 +258,26 @@
         cpack[c] = merge(acc[3 + c], cal[0, c], cal[1, c])
     cpack[1] = 0.25 * cpack[1]
 
-    def coefficients(x, carry):
-        here = mu[x + 1]
-        rate = RELAX_FACTOR / (6.0 * here + 3.0 * qb[x + 1])
-        half = 0.5 * rate
-        edge = at_edge(cpack[0], x)
-        near = (
-            z_next(here), z_prev(here), mu[x + 2], mu[x], y_next(here, edge), y_prev(here, edge),
-        )
-        rest = 1.0
-        for n, other in enumerate(near):
-            one = half * (here + other)
-            coef[n, x] = one
-            rest = rest - one
-        coef[6, x] = rest
-        coef[7, x] = rate
-        return carry
-
-    lax.fori_loop(0, bx, coefficients, 0)
+    def coefficients(x0):
+        found = []
+        for x in (x0, x0 + 1):
+            here = mu[x + 1]
+            rate = RELAX_FACTOR / (6.0 * here + 3.0 * qb[x + 1])
+            half = 0.5 * rate
+            edge = at_edge(cpack[0], x)
+            near = (
+                z_next(here), z_prev(here), mu[x + 2], mu[x], y_next(here, edge), y_prev(here, edge),
+            )
+            values = [half * (here + other) for other in near]
+            rest = 1.0
+            for one in values:
+                rest = rest - one
+            found.append(values + [rest, rate])
+        for u in range(2):
+            for n in range(8):
+                coef[n, x0 + u] = found[u][n]
+
+    pairs(0, bx, coefficients)
 
     def scale(x, carry):
         qb[x] = 0.25 * qb[x]
@@ -256,15 +285,38 @@
 
     lax.fori_loop(0, bx + 2, scale, 0)
 
-    def relax(p, got):
+    def relax(p, got_planes, got_packs):
         b, nb = p % 2, 1 - p % 2
         last = p == PASSES - 1
-        for arrive in got:
+        for arrive in got_packs[0]:
+            arrive()
+        for c in range(3):
+            packed[c] = merge(acc[c], al[p, 0, c], al[p, 1, c])
+
+        def gradient(at, edge):
+            vz, vy = field[b, 0, at + 1], field[b, 2, at + 1]
+            return qb[at] * (
+                (field[b, 1, at + 2] - field[b, 1, at])
+                + (z_next(vz) - z_prev(vz))
+                + (y_next(vy, edge) - y_prev(vy, edge))
+            )
+
+        def inner(x0):
+            pack = packed[2]
+            values = [gradient(x0 + u + 1, at_edge(pack, x0 + u)) for u in range(2)]
+            for u in range(2):
+                grad[x0 + u + 1] = values[u]
+
+        pairs(2, bx - 2, inner)
+        for arrive in got_planes:
             arrive()
         for c in range(3):
             field[b, c, 0:2] = xl[p, 0, c].astype(F32)
             field[b, c, bx + 2 : bx + 4] = xl[p, 1, c].astype(F32)
-            packed[c] = merge(acc[c], al[p, 0, c], al[p, 1, c])
+        inner(0)
+        inner(bx - 2)
+        for arrive in got_packs[1]:
+            arrive()
         corner = [[dl[p, k, c].astype(F32) for c in range(2)] for k in range(4)]
         top = GROUP * (bx - 1)
 
@@ -291,70 +343,71 @@
             + (pltpu.roll(vy, by - 2, 1) - pltpu.roll(vy, 2, 1))
         )
 
-        def gradient(at, edge):
-            vz, vy = field[b, 0, at + 1], field[b, 2, at + 1]
-            grad[at] = qb[at] * (
-                (field[b, 1, at + 2] - field[b, 1, at])
-                + (z_next(vz) - z_prev(vz))
-                + (y_next(vy, edge) - y_prev(vy, edge))
-            )
-
-        gradient(0, edge_corners(0, 1))
-        gradient(bx + 1, edge_corners(2, 3))
-
-        def inner(x, carry):
-            gradient(x + 1, at_edge(packed[2], x))
-            return carry
-
-        lax.fori_loop(0, bx, inner, 0)
+        low = gradient(0, edge_corners(0, 1))
+        high = gradient(bx + 1, edge_corners(2, 3))
+        grad[0] = low
+        grad[bx + 1] = high
         if not last:
             acc[0:3] = jnp.zeros((3, depth, by), F32)
 
-        def update(x, carry):
-            g = grad[x + 1]
-            g_edge = at_edge(packed[3], x)
-            rise = (
-                z_next(g) - z_prev(g),
-                grad[x + 2] - grad[x],
-                y_next(g, g_edge) - y_prev(g, g_edge),
-            )
-            k = [coef[n, x] for n in range(8)]
+        def update(x0):
+            news = [[], [], []]
+            for x in (x0, x0 + 1):
+                g = grad[x + 1]
+                g_edge = at_edge(packed[3], x)
+                rise = (
+                    z_next(g) - z_prev(g),
+                    grad[x + 2] - grad[x],
+                    y_next(g, g_edge) - y_prev(g, g_edge),
+                )
+                k = [coef[n, x] for n in range(8)]
+                for c in range(3):
+                    v = field[b, c, x + 2]
+                    edge = at_edge(packed[c], x)
+                    new = k[6] * v + k[7] * rise[c]
+                    new = new + k[0] * z_next(v) + k[1] * z_prev(v)
+                    new = new + k[2] * field[b, c, x + 3] + k[3] * field[b, c, x + 1]
+                    new = new + k[4] * y_next(v, edge) + k[5] * y_prev(v, edge)
+                    if p > 0:
+                        new = new + force[c, x]
+                    news[c].append(new)
             for c in range(3):
-                v = field[b, c, x + 2]
-                edge = at_edge(packed[c], x)
-                new = k[6] * v + k[7] * rise[c]
-                new = new + k[0] * z_next(v) + k[1] * z_prev(v)
-                new = new + k[2] * field[b, c, x + 3] + k[3] * field[b, c, x + 1]
-                new = new + k[4] * y_next(v, edge) + k[5] * y_prev(v, edge)
-                if p > 0:
-                    new = new + force[c, x]
-                if last:
-                    fout[c, strided(x), :] = new
-                else:
-                    field[nb, c, x + 2] = new
-                    if p > 0:
-                        pack_in(c, new, x)
-            return carry
-
-        lax.fori_loop(0, bx, update, 0)
-
-    relax(0, got_field)
+                for u in range(2):
+                    if last:
+                        fout[c, strided(x0 + u), :] = news[c][u]
+                    else:
+                        field[nb, c, x0 + u + 2] = news[c][u]
+                if p > 0 and not last:
+                    pack_in(c, news[c], x0)
+
+        if p == 0 or last:
+            pairs(0, bx, update)
+            return None
+        update(0)
+        update(bx - 2)
+        got_planes = send_planes(p + 1, nb)
+        pairs(2, bx - 2, update)
+        return got_planes, send_packs(p + 1)
+
+    relax(0, got_planes, got_packs)
 
     got_wy()
     wsum[...] = jnp.maximum(wq[0] + land_w[0] + land_wy[...], 1.0)
     acc[3] = jnp.zeros((depth, by), F32)
     tall[...] = tmpl[...].astype(F32)
 
-    def join(x, carry):
-        value = q00[x] + land_q[x, 0].astype(F32) + land_y[x].astype(F32)
-        plane = (value / wsum[pl.ds(x, 1), :]).astype(BF16).astype(F32)
-        joined[x + 1] = plane
-        pack_in(3, plane, x)
-        return carry
+    def join(x0):
+        planes = []
+        for x in (x0, x0 + 1):
+            value = q00[x] + land_q[x, 0].astype(F32) + land_y[x].astype(F32)
+            planes.append((value / wsum[pl.ds(x, 1), :]).astype(BF16).astype(F32))
+        for u in range(2):
+            joined[x0 + u + 1] = planes[u]
+        pack_in(3, planes, x0)
 
     for c in range(CHUNKS):
         got_y[c]()
-        lax.fori_loop(c * step, (c + 1) * step, join, 0)
+        pairs(c * step, (c + 1) * step, join)
     jxs[0] = joined[bx].astype(BF16)
     jxs[1] = joined[1].astype(BF16)
     jap[...] = acc[3].astype(BF16)
@@ -366,31 +419,40 @@
     joined[bx + 1] = jxl[1].astype(F32)
     cpack[0] = merge(acc[3], jal[0], jal[1])
 
-    def forcing(x, carry):
-        here = joined[x + 1]
-        edge = at_edge(cpack[0], x)
-        mismatch = (tall[strided(x), :] - here) * 0.5 * coef[7, x]
-        tall[strided(x), :] = here
-        slopes = (
-            z_next(here) - z_prev(here),
-            joined[x + 2] - joined[x],
-            y_next(here, edge) - y_prev(here, edge),
-        )
+    def forcing(x0):
+        span = (x0, x0 + 1)
+        ones, news, heres = [[], [], []], [[], [], []], []
+        for x in span:
+            here = joined[x + 1]
+            edge = at_edge(cpack[0], x)
+            mismatch = (tall[strided(x), :] - here) * 0.5 * coef[7, x]
+            slopes = (
+                z_next(here) - z_prev(here),
+                joined[x + 2] - joined[x],
+                y_next(here, edge) - y_prev(here, edge),
+            )
+            heres.append(here)
+            for c in range(3):
+                ones[c].append(mismatch * slopes[c])
+                news[c].append(field[1, c, x + 2] + ones[c][-1])
+        for u, x in enumerate(span):
+            tall[strided(x), :] = heres[u]
+            for c in range(3):
+                force[c, x] = ones[c][u]
+                field[1, c, x + 2] = news[c][u]
         for c in range(3):
-            one = mismatch * slopes[c]
-            force[c, x] = one
-            new = field[1, c, x + 2] + one
-            field[1, c, x + 2] = new
-            pack_in(c, new, x)
-        return carry
-
-    lax.fori_loop(0, bx, forcing, 0)
-    got_field = send_field(1, 1)
+            pack_in(c, news[c], x0)
+
+    forcing(0)
+    forcing(bx - 2)
+    got_planes = send_planes(1, 1)
+    pairs(2, bx - 2, forcing)
+    got_packs = send_packs(1)
     jout[...] = tall[...].astype(BF16)
     for p in range(1, PASSES):
-        relax(p, got_field)
-        if p < PASSES - 1:
-            got_field = send_field(p + 1, (p + 1) % 2)
+        sent = relax(p, got_planes, got_packs)
+        if sent is not None:
+            got_planes, got_packs = sent
     for src, dst, idx, d in pending:
         @pl.when(exists(d))
         def _(src=src, dst=dst, idx=idx, d=d):
@@ -405,6 +467,9 @@
     smem = pl.BlockSpec(memory_space=pltpu.SMEM)
     plane = (depth, by)
     shape = jax.ShapeDtypeStruct
+    table = jnp.concatenate(
+        [part.reshape(slots, -1).astype(F32) for part in (offset_x, offset_y, patch_wx)], axis=1
+    )
     quads = pl.pallas_call(
         blend_kernel,
         out_shape=(
@@ -413,20 +478,20 @@
             shape((bx,) + plane, BF16),
             shape((4, bx, by), F32),
         ),
-        in_specs=[smem] * 4 + [vmem] * 2,
+        in_specs=[smem] * 2 + [pl.BlockSpec(memory_space=pltpu.HBM), vmem],
         out_specs=(vmem,) * 4,
         scratch_shapes=[
             pltpu.VMEM((2, 2 * bx) + plane, F32),
             pltpu.VMEM((2, 2 * bx, 8, by), F32),
             pltpu.VMEM((2, depth * bx, by), F32),
+            pltpu.VMEM((slots, depth * bx, by), BF16),
+            pltpu.SemaphoreType.DMA((slots,)),
         ],
         compiler_params=pltpu.CompilerParams(vmem_limit_bytes=40 * 2**20),
         name="blend",
     )(
         block_counts,
-        offset_x.reshape(slots, 1),
-        offset_y.reshape(slots, 1),
-        patch_wx.reshape(slots, bx).astype(F32),
+        table,
         patches.reshape(slots, depth * bx, by),
         patch_wy,
     )

time: 83.6 us -> 73 us (0.87)
  the two profiles are of different devices: /device:TPU:0 before, /device:TPU:10 now
where the time goes in v1:
time: 73 us; the launch traced here: 71.9 us
  Pallas kernels  62.7 us (86%)
  local copies, waits for them, and re-layouts  5.81 us (8%)
  other arithmetic  2.07 us (3%)
  between operations  1.32 us (2%)
    pallas_call x1, Pallas kernels, per_device(): pl.pallas_call(relax_kernel, out_shape=(shape((depth * bx, by), BF16), sh...  58.6 us
    unnamed x11, local copies, waits for them, and re-layouts  5.64 us
    pallas_call x1, Pallas kernels, per_device(): pl.pallas_call(blend_kernel, out_shape=(shape((bx,) + plane, F32), shape(...  4.05 us
    convert_element_type x3, other arithmetic, per_device(): part.reshape(slots, -1).astype(F32)  2 us

profile of v1, /device:TPU:10, one launch (start us, length us, event | category | flops | bytes accessed | tf_op | source)
XLA Modules:
  0.0 71.9 jit_solution(5737078551065716165)
XLA Ops:
  1.3 0.7 convert_bitcast_fusion.1
  1.9 0.7 convert_bitcast_fusion
  2.6 0.1 copy.13
  2.7 0.1 copy.12
  2.8 0.7 bitcast_convert_fusion
  3.4 0.1 pad_maximum_fusion.table
  3.5 0.7 copy.14.wy_ref
  4.2 0.0 copy-start
  4.2 1.6 %copy-done = bf16[8,64,16,128]{3,2,1,0:T(8,128)(2,1)S(1)} copy-done((bf16[8,64,16,128]{3,2,1,0:T(8,128)(2,1)S(1)}, bf16[8,64,16,128]{3,2,1,0:T(8,128)(2,1)}, u32[]{:S(2)}) %copy-start) | copy-done | bytes 2097176
  5.8 0.0 copy-start.1
  5.8 0.0 copy-start.2
  5.8 0.0 copy-start.3
  5.8 4.0 %blend.1 = (f32[16,64,128]{2,1,0:T(8,128)S(1)}, bf16[16,2,64,128]{3,2,1,0:T(8,128)(2,1)S(1)}, bf16[16,64,128]{2,1,0:T(8,128)(2,1)S(1)}, f32[4,16,128]{2,1,0:T(8,128)S(1)}) custom-call(s32[1,1]{1,0:T(1,128)S(6)} %copy.17.count, f32[8,18]{1,0:T(8,128)S(1)} %pad_maximum_fusion.table, bf16[8,1024,128]{2,1,0:T(8,128)(2,1)S(1)} %bitcast.14, ...), custom_call_target="tpu_custom_call" | custom-call | tf_op jit(solution)/shard_map/blend/pallas_call | solution.py:473
  9.9 0.0 copy-done.1
  9.9 0.0 copy-done.2
  9.9 0.0 copy-done.3
  9.9 58.6 %relax.1 = (bf16[1024,128]{1,0:T(8,128)(2,1)S(1)}, f32[3,1024,128]{2,1,0:T(8,128)}) custom-call(f32[16,64,128]{2,1,0:T(8,128)S(1)} %get-tuple-element.8.q00, bf16[16,2,64,128]{3,2,1,0:T(8,128)(2,1)S(1)} %get-tuple-element.9.qx, bf16[16,64,128]{2,1,0:T(8,128)(2,1)S(1)} %get-tuple-element.10.q01, f32[4,16,128]{2,1,0:T(8,128)S(1)} %get-tuple-element.11.wq, ...), custom_call_target="tpu_custom_call" | custom-call | tf_op jit(solution)/shard_map/relax/pallas_call | solution.py:532
  68.5 0.7 copy.18
  69.2 2.7 %copy.19 = f32[3,64,16,128]{3,2,1,0:T(8,128)} copy(f32[3,64,16,128]{3,2,1,0:T(8,128)} %bitcast.20) | data formatting | bytes 3145728
Async XLA Ops:
  4.2 1.6 %copy-start = (bf16[8,64,16,128]{3,2,1,0:T(8,128)(2,1)S(1)}, bf16[8,64,16,128]{3,2,1,0:T(8,128)(2,1)}, u32[]{:S(2)}) copy-start(bf16[8,64,16,128]{3,2,1,0:T(8,128)(2,1)} %param.10) | copy-start | bytes 6291460
  5.8 4.1 %copy-start.1 = (f32[64,16,128]{2,1,0:T(8,128)S(1)}, f32[64,16,128]{2,1,0:T(8,128)}, u32[]{:S(2)}) copy-start(f32[64,16,128]{2,1,0:T(8,128)} %param.17) | copy-start | bytes 1572868
  5.8 4.1 %copy-start.2 = (f32[64,16,128]{2,1,0:T(8,128)S(1)}, f32[64,16,128]{2,1,0:T(8,128)}, u32[]{:S(2)}) copy-start(f32[64,16,128]{2,1,0:T(8,128)} %param.18) | copy-start | bytes 1572868
  5.8 4.1 %copy-start.3 = (bf16[64,16,128]{2,1,0:T(8,128)(2,1)S(1)}, bf16[64,16,128]{2,1,0:T(8,128)(2,1)}, u32[]{:S(2)}) copy-start(bf16[64,16,128]{2,1,0:T(8,128)(2,1)} %param.16) | copy-start | bytes 786436

commit v2 on v1

--- a/solution.py
+++ b/solution.py
@@ -17,7 +17,7 @@
 GROUP = 8
 
 
-def blend_kernel(count, table, patches, wy_ref, q00, qx, q01, wout, canvas, wcan, res, held, arrived):
+def blend_kernel(count, ox_ref, oy_ref, patches, wx_ref, wy_ref, q00, qx, q01, wout, canvas, wcan, res, held, wxf, wyf, arrived):
     by = held.shape[-1]
     bx, depth = q00.shape[:2]
     live = count[0, 0]
@@ -32,25 +32,33 @@
     lax.fori_loop(0, live, begin, 0)
     canvas[...] = jnp.zeros_like(canvas)
     wcan[...] = jnp.zeros_like(wcan)
+    wxf[...] = wx_ref[...].astype(F32)
+    wyf[...] = wy_ref[...].astype(F32)
     source = lax.broadcasted_iota(jnp.int32, (by, 2 * by), 0)
     target = lax.broadcasted_iota(jnp.int32, (by, 2 * by), 1)
 
     def add_patch(s, carry):
-        ox = table[s, 0].astype(jnp.int32)
-        oy = table[s, 1].astype(jnp.int32)
-        place = jnp.where(target == source + oy, 1.0, 0.0).astype(BF16)
+        ox = ox_ref[0, s]
+        place = jnp.where(target == source + oy_ref[0, s], 1.0, 0.0).astype(BF16)
         fetch(s).wait()
         moved = jnp.dot(held[s], place, preferred_element_type=F32)
         res[0] = moved[:, :by]
         res[1] = moved[:, by:]
-        along_y = jnp.broadcast_to(wy_ref[s].astype(F32), (16, by)).astype(BF16)
+        along_y = jnp.broadcast_to(wyf[pl.ds(s, 1), :], (16, by)).astype(BF16)
         wy_row = jnp.dot(along_y, place, preferred_element_type=F32)[:8]
-        for x in range(bx):
-            wx = table[s, 2 + x]
+        along_x = jnp.broadcast_to(wxf[pl.ds(s, 1), :], (8, bx))
+        for x0 in range(0, bx, 4):
             for h in range(2):
-                weight = wx * wy_row[:, h * by : (h + 1) * by]
-                canvas[h, ox + x] += res[h, pl.ds(x, depth, stride=bx), :] * weight[0:1]
-                wcan[h, ox + x] += weight
+                span = range(x0, x0 + 4)
+                weights = [along_x[:, x : x + 1] * wy_row[:, h * by : (h + 1) * by] for x in span]
+                sums = [
+                    canvas[h, ox + x] + res[h, pl.ds(x, depth, stride=bx), :] * weight[0:1]
+                    for x, weight in zip(span, weights)
+                ]
+                totals = [wcan[h, ox + x] + weight for x, weight in zip(span, weights)]
+                for n, x in enumerate(span):
+                    canvas[h, ox + x] = sums[n]
+                    wcan[h, ox + x] = totals[n]
         return carry
 
     lax.fori_loop(0, live, add_patch, 0)
@@ -168,14 +176,6 @@
             pl.semaphore_signal(barrier, inc=1, device_id=(gx + d[0], gy + d[1]), device_id_type=MESH)
 
         total = total + jnp.where(exists(d), 1, 0)
-    pl.semaphore_wait(barrier, total)
-
-    step = bx // CHUNKS
-    got_q = []
-    for c in range(CHUNKS):
-        part = pl.ds(c * step, step)
-        got_q.append(send(qx.at[part], land_q.at[part], (1, 0)))
-    got_w = send(wq.at[pl.ds(1, 2)], land_w, (1, 0))
 
     for k, d in enumerate(DIRS):
         @pl.when(jnp.logical_not(exists(opposite(d))))
@@ -201,12 +201,20 @@
                     dl[p, k - 4] = jnp.zeros(dl.shape[2:], BF16)
 
     acc[...] = jnp.zeros_like(acc)
+    pl.semaphore_wait(barrier, total)
+
+    step = bx // CHUNKS
+    got_q = []
+    for c in range(CHUNKS):
+        part = pl.ds(c * step, step)
+        got_q.append(send(qx.at[part], land_q.at[part], (1, 0)))
+    got_w = send(wq.at[pl.ds(1, 2)], land_w, (1, 0))
 
     def load(x0):
         span = (x0, x0 + 1)
         planes = [[fld[c, strided(x), :] for x in span] for c in range(3)]
         mus = [mu_ref[strided(x), :] for x in span]
-        bulks = [lam_ref[strided(x), :] + one for x, one in zip(span, mus)]
+        bulks = [0.25 * (lam_ref[strided(x), :] + one) for x, one in zip(span, mus)]
         for u, x in enumerate(span):
             for c in range(3):
                 field[0, c, x + 2] = planes[c][u]
@@ -243,11 +251,15 @@
     sw[...] = wq[3] + land_w[1]
     got_wy = send(sw, land_wy, (0, 1))
     got_y = []
-    for c in range(CHUNKS):
+
+    def pass_on(c):
         part = pl.ds(c * step, step)
         got_q[c]()
         sy[part] = (q01[part].astype(F32) + land_q[part, 1].astype(F32)).astype(BF16)
         got_y.append(send(sy.at[part], land_y.at[part], (0, 1)))
+
+    for c in range(CHUNKS // 2):
+        pass_on(c)
 
     for arrive in got_coef:
         arrive()
@@ -256,13 +268,12 @@
         qb[at] = cxl[k, 1].astype(F32)
     for c in range(2):
         cpack[c] = merge(acc[3 + c], cal[0, c], cal[1, c])
-    cpack[1] = 0.25 * cpack[1]
 
     def coefficients(x0):
         found = []
         for x in (x0, x0 + 1):
             here = mu[x + 1]
-            rate = RELAX_FACTOR / (6.0 * here + 3.0 * qb[x + 1])
+            rate = RELAX_FACTOR / (6.0 * here + 12.0 * qb[x + 1])
             half = 0.5 * rate
             edge = at_edge(cpack[0], x)
             near = (
@@ -278,12 +289,8 @@
                 coef[n, x0 + u] = found[u][n]
 
     pairs(0, bx, coefficients)
-
-    def scale(x, carry):
-        qb[x] = 0.25 * qb[x]
-        return carry
-
-    lax.fori_loop(0, bx + 2, scale, 0)
+    for c in range(CHUNKS // 2, CHUNKS):
+        pass_on(c)
 
     def relax(p, got_planes, got_packs):
         b, nb = p % 2, 1 - p % 2
@@ -301,20 +308,23 @@
                 + (y_next(vy, edge) - y_prev(vy, edge))
             )
 
-        def inner(x0):
+        def inner(span):
             pack = packed[2]
-            values = [gradient(x0 + u + 1, at_edge(pack, x0 + u)) for u in range(2)]
-            for u in range(2):
-                grad[x0 + u + 1] = values[u]
-
-        pairs(2, bx - 2, inner)
+            values = [gradient(x + 1, at_edge(pack, x)) for x in span]
+            for x, value in zip(span, values):
+                grad[x + 1] = value
+
+        def four(n, carry):
+            inner([2 + 4 * n + u for u in range(4)])
+            return carry
+
+        lax.fori_loop(0, (bx - 4) // 4, four, 0)
         for arrive in got_planes:
             arrive()
         for c in range(3):
             field[b, c, 0:2] = xl[p, 0, c].astype(F32)
             field[b, c, bx + 2 : bx + 4] = xl[p, 1, c].astype(F32)
-        inner(0)
-        inner(bx - 2)
+        inner([0, 1, bx - 2, bx - 1])
         for arrive in got_packs[1]:
             arrive()
         corner = [[dl[p, k, c].astype(F32) for c in range(2)] for k in range(4)]
@@ -467,9 +477,6 @@
     smem = pl.BlockSpec(memory_space=pltpu.SMEM)
     plane = (depth, by)
     shape = jax.ShapeDtypeStruct
-    table = jnp.concatenate(
-        [part.reshape(slots, -1).astype(F32) for part in (offset_x, offset_y, patch_wx)], axis=1
-    )
     quads = pl.pallas_call(
         blend_kernel,
         out_shape=(
@@ -478,22 +485,26 @@
             shape((bx,) + plane, BF16),
             shape((4, bx, by), F32),
         ),
-        in_specs=[smem] * 2 + [pl.BlockSpec(memory_space=pltpu.HBM), vmem],
+        in_specs=[smem] * 3 + [pl.BlockSpec(memory_space=pltpu.HBM), vmem, vmem],
         out_specs=(vmem,) * 4,
         scratch_shapes=[
             pltpu.VMEM((2, 2 * bx) + plane, F32),
             pltpu.VMEM((2, 2 * bx, 8, by), F32),
             pltpu.VMEM((2, depth * bx, by), F32),
             pltpu.VMEM((slots, depth * bx, by), BF16),
+            pltpu.VMEM((slots, bx), F32),
+            pltpu.VMEM((slots, by), F32),
             pltpu.SemaphoreType.DMA((slots,)),
         ],
         compiler_params=pltpu.CompilerParams(vmem_limit_bytes=40 * 2**20),
         name="blend",
     )(
         block_counts,
-        table,
+        offset_x.reshape(1, slots),
+        offset_y.reshape(1, slots),
         patches.reshape(slots, depth * bx, by),
-        patch_wy,
+        patch_wx.reshape(slots, bx),
+        patch_wy.reshape(slots, by),
     )
     n_copies = CHUNKS + 1 + 8 + 4 + 1 + CHUNKS + 4 + 8 * (PASSES - 1)
     scratch = [

time: 73 us -> 72.1 us (0.988)
  the two profiles are of different devices: /device:TPU:10 before, /device:TPU:0 now
where the time goes in v2:
time: 72.1 us; the launch traced here: 71.2 us
  Pallas kernels  62.2 us (86%)
  local copies, waits for them, and re-layouts  7.62 us (11%)
  between operations  1.33 us (2%)
    pallas_call x1, Pallas kernels, per_device(): pl.pallas_call(relax_kernel, out_shape=(shape((depth * bx, by), BF16), sh...  58.2 us
    unnamed x18, local copies, waits for them, and re-layouts  7.62 us
    pallas_call x1, Pallas kernels, per_device(): pl.pallas_call(blend_kernel, out_shape=(shape((bx,) + plane, F32), shape(...  4.04 us

profile of v2, /device:TPU:0, one launch (start us, length us, event | category | flops | bytes accessed | tf_op | source)
XLA Modules:
  0.0 71.2 jit_solution(15759486638788569029)
XLA Ops:
  1.3 0.0 copy-start
  1.3 1.6 %copy-done = bf16[8,64,16,128]{3,2,1,0:T(8,128)(2,1)S(1)} copy-done((bf16[8,64,16,128]{3,2,1,0:T(8,128)(2,1)S(1)}, bf16[8,64,16,128]{3,2,1,0:T(8,128)(2,1)}, u32[]{:S(2)}) %copy-start) | copy-done | bytes 2097176
  2.9 0.0 copy-start.4
  2.9 0.7 copy-done.4
  3.6 0.0 copy-start.5
  3.6 0.7 copy-done.5
  4.2 0.0 copy-start.6
  4.2 0.7 copy-done.6
  4.9 0.0 copy-start.7
  4.9 0.7 copy-done.7
  5.5 0.0 copy-start.1
  5.5 0.0 copy-start.2
  5.5 0.0 copy-start.3
  5.6 4.0 %blend.1 = (f32[16,64,128]{2,1,0:T(8,128)S(1)}, bf16[16,2,64,128]{3,2,1,0:T(8,128)(2,1)S(1)}, bf16[16,64,128]{2,1,0:T(8,128)(2,1)S(1)}, f32[4,16,128]{2,1,0:T(8,128)S(1)}) custom-call(s32[1,1]{1,0:T(1,128)S(6)} %copy.14.count, s32[1,8]{1,0:T(1,128)S(1)} %bitcast.18, s32[1,8]{1,0:T(1,128)S(1)} %bitcast.19, bf16[8,1024,128]{2,1,0:T(8,128)(2,1)S(1)} %bitcast.11, ...), custom_call_target="tpu_custom_call" | custom-call | tf_op jit(solution)/shard_map/blend/pallas_call | solution.py:480
  9.6 0.0 copy-done.1
  9.6 0.0 copy-done.2
  9.6 0.0 copy-done.3
  9.6 58.2 %relax.1 = (bf16[1024,128]{1,0:T(8,128)(2,1)S(1)}, f32[3,1024,128]{2,1,0:T(8,128)}) custom-call(f32[16,64,128]{2,1,0:T(8,128)S(1)} %get-tuple-element.8.q00, bf16[16,2,64,128]{3,2,1,0:T(8,128)(2,1)S(1)} %get-tuple-element.9.qx, bf16[16,64,128]{2,1,0:T(8,128)(2,1)S(1)} %get-tuple-element.10.q01, f32[4,16,128]{2,1,0:T(8,128)S(1)} %get-tuple-element.11.wq, ...), custom_call_target="tpu_custom_call" | custom-call | tf_op jit(solution)/shard_map/relax/pallas_call | solution.py:543
  67.8 0.7 copy.15
  68.5 2.7 %copy.16 = f32[3,64,16,128]{3,2,1,0:T(8,128)} copy(f32[3,64,16,128]{3,2,1,0:T(8,128)} %bitcast.21) | data formatting | bytes 3145728
Async XLA Ops:
  1.3 1.6 %copy-start = (bf16[8,64,16,128]{3,2,1,0:T(8,128)(2,1)S(1)}, bf16[8,64,16,128]{3,2,1,0:T(8,128)(2,1)}, u32[]{:S(2)}) copy-start(bf16[8,64,16,128]{3,2,1,0:T(8,128)(2,1)} %param.10) | copy-start | bytes 6291460
  2.9 0.7 copy-start.4
  3.6 0.7 copy-start.5
  4.2 0.7 copy-start.6
  4.9 0.7 copy-start.7
  5.5 4.1 %copy-start.1 = (f32[64,16,128]{2,1,0:T(8,128)S(1)}, f32[64,16,128]{2,1,0:T(8,128)}, u32[]{:S(2)}) copy-start(f32[64,16,128]{2,1,0:T(8,128)} %param.17) | copy-start | bytes 1572868
  5.5 4.1 %copy-start.2 = (f32[64,16,128]{2,1,0:T(8,128)S(1)}, f32[64,16,128]{2,1,0:T(8,128)}, u32[]{:S(2)}) copy-start(f32[64,16,128]{2,1,0:T(8,128)} %param.18) | copy-start | bytes 1572868
  5.5 4.1 %copy-start.3 = (bf16[64,16,128]{2,1,0:T(8,128)(2,1)S(1)}, bf16[64,16,128]{2,1,0:T(8,128)(2,1)}, u32[]{:S(2)}) copy-start(bf16[64,16,128]{2,1,0:T(8,128)(2,1)} %param.16) | copy-start | bytes 786436

commit v3 on v2

--- a/solution.py
+++ b/solution.py
@@ -496,7 +496,7 @@
             pltpu.VMEM((slots, by), F32),
             pltpu.SemaphoreType.DMA((slots,)),
         ],
-        compiler_params=pltpu.CompilerParams(vmem_limit_bytes=40 * 2**20),
+        compiler_params=pltpu.CompilerParams(vmem_limit_bytes=62 * 2**20),
         name="blend",
     )(
         block_counts,
@@ -548,7 +548,7 @@
         scratch_shapes=[pltpu.VMEM(dims, kind) for dims, kind in scratch]
         + [pltpu.SemaphoreType.DMA((n_copies,)), pltpu.SemaphoreType.DMA((n_copies,))],
         compiler_params=pltpu.CompilerParams(
-            collective_id=0, has_side_effects=True, vmem_limit_bytes=50 * 2**20
+            collective_id=0, has_side_effects=True, vmem_limit_bytes=62 * 2**20
         ),
         name="relax",
     )(

time: 72.1 us -> 70.5 us (0.978)
  local copies, waits for them, and re-layouts: 7.62 us -> 4.32 us
  Pallas kernels: 62.2 us -> 64.6 us
    unnamed x18 -> x2, local copies, waits for them, and re-layouts: 7.62 us -> 4.32 us
    pallas_call x1, Pallas kernels: 58.2 us -> 60.2 us  [per_device(): pl.pallas_call(relax_kernel, out_shape=(shape((depth * bx, by), BF16), sh...]
where the time goes in v3:
time: 70.5 us; the launch traced here: 70.2 us
  Pallas kernels  64.6 us (92%)
  local copies, waits for them, and re-layouts  4.32 us (6%)
  between operations  1.29 us (2%)
    pallas_call x1, Pallas kernels, per_device(): pl.pallas_call(relax_kernel, out_shape=(shape((depth * bx, by), BF16), sh...  60.2 us
    pallas_call x1, Pallas kernels, per_device(): pl.pallas_call(blend_kernel, out_shape=(shape((bx,) + plane, F32), shape(...  4.34 us
    unnamed x2, local copies, waits for them, and re-layouts  4.32 us

profile of v3, /device:TPU:0, one launch (start us, length us, event | category | flops | bytes accessed | tf_op | source)
XLA Modules:
  0.0 70.2 jit_solution(12662724754754649367)
XLA Ops:
  1.3 4.3 %blend.1 = (f32[16,64,128]{2,1,0:T(8,128)}, bf16[16,2,64,128]{3,2,1,0:T(8,128)(2,1)}, bf16[16,64,128]{2,1,0:T(8,128)(2,1)}, f32[4,16,128]{2,1,0:T(8,128)}) custom-call(s32[1,1]{1,0:T(1,128)S(6)} %copy.14.count, s32[1,8]{1,0:T(1,128)} %bitcast.20, s32[1,8]{1,0:T(1,128)} %bitcast.21, bf16[8,1024,128]{2,1,0:T(8,128)(2,1)} %bitcast.11, bf16[8,16]{1,0:T(8,128)(2,1)} %bitcast.18, ...), custom_call_target="tpu_custom_call" | custom-call | tf_op jit(solution)/shard_map/blend/pallas_call | solution.py:480
  5.6 60.2 %relax.1 = (bf16[1024,128]{1,0:T(8,128)(2,1)}, f32[3,1024,128]{2,1,0:T(8,128)}) custom-call(f32[16,64,128]{2,1,0:T(8,128)} %get-tuple-element.8.q00, bf16[16,2,64,128]{3,2,1,0:T(8,128)(2,1)} %get-tuple-element.9.qx, bf16[16,64,128]{2,1,0:T(8,128)(2,1)} %get-tuple-element.10.q01, f32[4,16,128]{2,1,0:T(8,128)} %get-tuple-element.11.wq, ...), custom_call_target="tpu_custom_call" | custom-call | tf_op jit(solution)/shard_map/relax/pallas_call | solution.py:543
  65.9 1.7 %copy.15 = bf16[64,16,128]{2,1,0:T(8,128)(2,1)} copy(bf16[64,16,128]{2,1,0:T(8,128)(2,1)} %bitcast.17) | data formatting | bytes 524288
  67.5 2.7 %copy.16 = f32[3,64,16,128]{3,2,1,0:T(8,128)} copy(f32[3,64,16,128]{3,2,1,0:T(8,128)} %bitcast.13) | data formatting | bytes 3145728
